TPU v7x, 32 devices: a whole 2x2x4 slice. The times are simulated.
32 devices in a mesh: src: 8 (over z, x), tgt: 4 (over y, core).
Axes of the slice: x: 2, y: 2, z: 4, core: 2. Of those that a mesh axis runs over, the one named last changes fastest.
Arguments:
- src_embed: float32 [16384, 256], P(('src', 'tgt')), may hold values from -7.5 to 7.5
- tgt_embed: float32 [16384, 256], P(('tgt', 'src')), may hold values from -7.5 to 7.5
- log_src: float32 [16384], P('src'), may hold values from -1.25 to 2.35
- log_tgt: float32 [16384], P('tgt'), may hold values from -1.25 to 2.35
- tgt_pot: float32 [16384], P('tgt'), may hold values from -1 to 6
Outputs:
- src_dual: float32 [16384], P('src')
- tgt_dual: float32 [16384], P('tgt')
All inputs are finite; a program needn't handle non-finite values.
Results may differ from a plain program's by a relative error of at most 0.0003.
Values sent between devices are 32-bit elements; how exact they have to be, the bound alone decides.
A program may use at most 128 MiB of HBM per device.

v0:
```python
import jax
import jax.numpy as jnp
from jax import lax
from jax.sharding import PartitionSpec as P

EPSILON = 0.05


def combined_all(shard, axis, combine):
    everything = jax.tree.map(lambda part: lax.all_gather(part, axis), shard)
    initial = jax.tree.map(lambda part: part[0], everything)

    def turn(k, so_far):
        return combine(so_far, jax.tree.map(lambda part: part[k], everything))

    return lax.fori_loop(1, lax.axis_size(axis), turn, initial)


def pair_combine(first, second):
    top = jnp.maximum(first[0], second[0])
    return (top, first[1] * jnp.exp(first[0] - top) + second[1] * jnp.exp(second[0] - top))


def cross_inner(left, right):
    return lax.dot_general(
        left,
        right,
        (((1,), (1,)), ((), ())),
        precision=lax.Precision.HIGHEST,
        preferred_element_type=jnp.float32,
    )


def row_lse(scores):
    local_top = jnp.max(scores, axis=1)
    local_sum = jnp.sum(jnp.exp(scores - local_top[:, None]), axis=1)
    highest, totals = combined_all((local_top, local_sum), "tgt", pair_combine)
    return highest + jnp.log(totals)


def column_lse(scores):
    local_top = jnp.max(scores, axis=0)
    local_sum = jnp.sum(jnp.exp(scores - local_top[None, :]), axis=0)
    highest, totals = combined_all((local_top, local_sum), "src", pair_combine)
    return highest + jnp.log(totals)


def shards(src_embed, tgt_embed, log_src, log_tgt, tgt_pot):
    width = src_embed.shape[1]
    targets = lax.all_gather(tgt_embed, "src", axis=0, tiled=True)
    tgt_norm = jnp.sum(targets * targets, axis=1)
    piece = lax.all_gather(src_embed, "tgt", axis=0, tiled=True)
    src_norm = jnp.sum(piece * piece, axis=1)
    cost = (src_norm[:, None] + tgt_norm[None, :] - 2.0 * cross_inner(piece, targets)) / width
    tgt_dual = tgt_pot
    src_dual = -EPSILON * row_lse(log_tgt[None, :] + (tgt_dual[None, :] - cost) / EPSILON)
    tgt_dual = -EPSILON * column_lse(log_src[:, None] + (src_dual[:, None] - cost) / EPSILON)
    return (src_dual, tgt_dual)


def solution(mesh):
    in_specs = (P(("src", "tgt"), None), P(("tgt", "src"), None), P("src"), P("tgt"), P("tgt"))
    out_specs = (P("src"), P("tgt"))
    return jax.shard_map(shards, mesh=mesh, in_specs=in_specs, out_specs=out_specs, check_vma=False)
```

profile of v0, /device:TPU:0, one launch (start us, length us, event | category | flops | bytes accessed | tf_op | source)
XLA Modules:
  0.0 278.6 jit_solution(8682660193862429845)
XLA Ops:
  7.2 0.0 all-gather.7.cloned.1.call-start
  7.2 0.7 all-gather.7.cloned.1.call-update
  7.9 0.0 all-gather.9.cloned.1.call-start
  7.9 0.7 all-gather.9.cloned.1.call-update
  8.6 26.2 %all-gather.7.cloned.1.call-done = f32[2048,256]{1,0:T(8,128)} async-done(((f32[512,256]{1,0:T(8,128)}), f32[2048,256]{1,0:T(8,128)}) %all-gather.7.cloned.1.call-update) | async-done | bytes 2097168 | tf_op jit(solution)/shard_map/all_gather | solution.py:52
  34.9 1.9 multiply_reduce_fusion.1
  36.8 73.6 %all-gather.9.cloned.1.call-done = f32[4096,256]{1,0:T(8,128)} async-done(((f32[512,256]{1,0:T(8,128)}), f32[4096,256]{1,0:T(8,128)}) %all-gather.9.cloned.1.call-update) | async-done | bytes 4194320 | tf_op jit(solution)/shard_map/all_gather | solution.py:50
  110.4 2.8 %multiply_reduce_fusion = f32[4096]{0:T(1024)S(1)} fusion(f32[4096,256]{1,0:T(8,128)} %all-gather.9.cloned.1.call-done), kind=kLoop, calls=%fused_computation.13 | loop fusion | flops 2093056 | bytes 4210688 | tf_op jit(solution)/shard_map/reduce_sum | solution.py:51
  113.2 0.0 copy-start.2
  113.3 0.0 copy-start.3
  113.3 41.2 %fusion = (f32[2048]{0:T(1024)S(1)}, f32[2048,4096]{1,0:T(8,128)}) fusion(f32[4096]{0:T(1024)} %param.13, f32[4096]{0:T(1024)} %param.12, f32[2048,256]{1,0:T(8,128)} %all-gather.7.cloned.1.call-done, f32[4096,256]{1,0:T(8,128)} %all-gather.9.cloned.1.call-done, f32[4096]{0:T(1024)S(1)} %multiply_reduce_fusion, f32[2048]{0:T(1024)S(1)} %multiply_reduce_fusion.1), kind=kOutput, calls=%fused_computation.11 | convolution fusion | flops 25836910592 | bytes 39911424 | tf_op jit(solution)/shard_map/dot_general | solution.py:25
  154.5 0.0 copy-done.2
  154.5 0.0 copy-done.3
  154.5 15.2 %exponential_reduce_fusion.1 = f32[2048]{0:T(1024)S(1)} fusion(f32[2048,4096]{1,0:T(8,128)} %get-tuple-element.301, f32[2048]{0:T(1024)S(1)} %get-tuple-element.300, f32[4096]{0:T(1024)S(1)} %copy-done.2, f32[4096]{0:T(1024)S(1)} %copy-done.3), kind=kLoop, calls=%fused_computation.8 | loop fusion | flops 41940992 | bytes 33603584 | tf_op jit(solution)/shard_map/reduce_sum | solution.py:36
  169.6 5.4 %all-gather.1 = f32[8192]{0:T(1024)S(1)} all-gather(f32[2048]{0:T(1024)S(1)} %exponential_reduce_fusion.1), channel_id=3, replica_groups=mesh['src'=8,'tgt'=4] {'tgt'}, dimensions={0}, use_global_device_ids=true | all-gather | bytes 40960 | tf_op jit(solution)/shard_map/all_gather | solution.py:10
  175.0 5.2 %all-gather = f32[8192]{0:T(1024)S(1)} all-gather(f32[2048]{0:T(1024)S(1)} %get-tuple-element.300), channel_id=2, replica_groups=mesh['src'=8,'tgt'=4] {'tgt'}, dimensions={0}, use_global_device_ids=true | all-gather | bytes 40960 | tf_op jit(solution)/shard_map/all_gather | solution.py:10
  180.3 0.2 while.34
  180.5 0.0 copy-start
  180.5 13.7 %fusion.1 = f32[4096]{0:T(1024)S(1)} fusion(f32[2048,4096]{1,0:T(8,128)} %get-tuple-element.301, f32[2048]{0:T(1024)S(1)} %add_multiply_fusion.1, f32[2048]{0:T(1024)S(1)} %copy-done.1), kind=kLoop, calls=%fused_computation.12 | loop fusion | flops 33550336 | bytes 33587200 | tf_op jit(solution)/shard_map/reduce_max | solution.py:42
  194.2 15.1 %exponential_reduce_fusion = f32[4096]{0:T(1024)S(1)} fusion(f32[2048,4096]{1,0:T(8,128)} %get-tuple-element.301, f32[4096]{0:T(1024)S(1)} %fusion.1, f32[2048]{0:T(1024)S(1)} %add_multiply_fusion.1, f32[2048]{0:T(1024)S(1)} %copy-done.1), kind=kLoop, calls=%fused_computation.6 | loop fusion | flops 41938944 | bytes 33603584 | tf_op jit(solution)/shard_map/reduce_sum | solution.py:43
  209.3 30.6 %all-gather.3 = f32[32768]{0:T(1024)S(1)} all-gather(f32[4096]{0:T(1024)S(1)} %exponential_reduce_fusion), channel_id=5, replica_groups=mesh['src'=8,'tgt'=4] {'src'}, dimensions={0}, use_global_device_ids=true | all-gather | bytes 147456 | tf_op jit(solution)/shard_map/all_gather | solution.py:10
  240.0 30.5 %all-gather.2 = f32[32768]{0:T(1024)S(1)} all-gather(f32[4096]{0:T(1024)S(1)} %fusion.1), channel_id=4, replica_groups=mesh['src'=8,'tgt'=4] {'src'}, dimensions={0}, use_global_device_ids=true | all-gather | bytes 147456 | tf_op jit(solution)/shard_map/all_gather | solution.py:10
  270.5 0.6 while.35
  271.1 0.6 add_multiply_fusion
  (32 shorter events, 0.6 us)
Async XLA Ops:
  7.2 27.7 %all-gather.7.cloned.1.call-start = ((), (), s32[]{:S(2)}) async-start(), calls=%async_computation | async-start | bytes 2621440 | tf_op jit(solution)/shard_map/all_gather | solution.py:52
  7.9 102.5 %all-gather.9.cloned.1.call-start = ((), (), s32[]{:S(2)}) async-start(), calls=%async_computation.1 | async-start | bytes 4718592 | tf_op jit(solution)/shard_map/all_gather | solution.py:50
  113.2 41.2 %copy-start.2 = (f32[4096]{0:T(1024)S(1)}, f32[4096]{0:T(1024)}, u32[]{:S(2)}) copy-start(f32[4096]{0:T(1024)} %param.13) | copy-start | bytes 49156
  113.3 41.2 %copy-start.3 = (f32[4096]{0:T(1024)S(1)}, f32[4096]{0:T(1024)}, u32[]{:S(2)}) copy-start(f32[4096]{0:T(1024)} %param.12) | copy-start | bytes 49156
  154.5 26.0 %copy-start.1 = (f32[2048]{0:T(1024)S(1)}, f32[2048]{0:T(1024)}, u32[]{:S(2)}) copy-start(f32[2048]{0:T(1024)} %param.11) | copy-start | bytes 24580
  180.5 28.8 %copy-start = (f32[2048]{0:T(1024)}, f32[2048]{0:T(1024)S(1)}, u32[]{:S(2)}) copy-start(f32[2048]{0:T(1024)S(1)} %add_multiply_fusion.1) | copy-start | bytes 24580
Sparse Core Ops, SparseCore 0:
  9.6 25.2 all-gather.6
  37.0 73.3 all-gather.8
where the time goes:
time: 279 us
  waiting for transfers between devices  101 us (36%)
  blocking collectives  71.7 us (26%)
  other arithmetic  49.5 us (18%)
  matrix products  41.2 us (15%)
  between operations  14.2 us (5%)
    all_gather x1, waiting for transfers between devices, shards(): targets = lax.all_gather(tgt_embed, 'src', axis=0, tiled=True)  73.6 us
    all_gather x4, blocking collectives, combined_all(): everything = jax.tree.map(lambda part: lax.all_gather(part, axis), shard)  71.7 us
    dot_general x1, matrix products, cross_inner(): lax.dot_general(left, right, (((1,), (1,)), ((), ())), precision=lax.Prec...  41.2 us
    all_gather x1, waiting for transfers between devices, shards(): piece = lax.all_gather(src_embed, 'tgt', axis=0, tiled=True)  26.2 us
    reduce_sum x1, other arithmetic, row_lse(): local_sum = jnp.sum(jnp.exp(scores - local_top[:, None]), axis=1)  15.2 us
    reduce_sum x1, other arithmetic, column_lse(): local_sum = jnp.sum(jnp.exp(scores - local_top[None, :]), axis=0)  15.1 us
    reduce_max x1, other arithmetic, column_lse(): local_top = jnp.max(scores, axis=0)  13.7 us
  transfers between devices with their start and end apart: 2, of which 2 were waited for; matrix products, arithmetic and copies ran while one was open for 1% of the time, Pallas kernels for 0%

commit v1 on v0

v1 whole, which is shorter than its diff:
```python
import functools
import math

import jax
import jax.numpy as jnp
from jax import lax
from jax.experimental import pallas as pl
from jax.experimental.pallas import tpu as pltpu
from jax.sharding import PartitionSpec as P

EPSILON = 0.05
LOG2E = math.log2(math.e)
LN2 = math.log(2.0)
LOW = -1e38
LANES = 128
CHUNKS = 2


def ring_place(src, wide, deep):
    z, x = src // wide, src % wide
    return x * deep + jnp.where(x % 2 == 0, z, deep - 1 - z)


def ring_owner(place, wide, deep):
    x, step = place // deep, place % deep
    z = jnp.where(x % 2 == 0, step, deep - 1 - step)
    return z * wide + x


def across(column, count):
    return jnp.concatenate([column] * (count // LANES), axis=1)


def upright(row):
    return jnp.transpose(jnp.broadcast_to(row, (LANES, row.shape[1])))


def flat(columns):
    return jnp.transpose(columns)[0:1, :]


def halves(values):
    high = values.astype(jnp.bfloat16)
    low = (values - high.astype(jnp.float32)).astype(jnp.bfloat16)
    return high, low


def contract(left, right):
    return lax.dot_general(
        left, right, (((1,), (1,)), ((), ())), preferred_element_type=jnp.float32
    )


def combine(parts, count):
    top = functools.reduce(jnp.maximum, [parts[k] for k in range(count)])
    total = sum(jnp.exp2(parts[k] - top) for k in range(count))
    return top + jnp.log2(total)


def kernel(
    n_src, n_tgt, wide, deep,
    x_own, y_own, log_src, log_tgt, pot, src_out, tgt_out,
    x_all, y_all, x_ops, y_ops, a_col, b_col, x_norm, y_norm,
    row_top, row_sum, row_parts, col_parts,
    ring_send, ring_recv, y_send, y_recv, core_send, core_recv,
    row_send, row_recv, col_send, col_recv,
):
    s = lax.axis_index("src")
    t = lax.axis_index("tgt")
    n_y = n_tgt // 2
    y_me, core = t // 2, t % 2
    partner = y_me * 2 + 1 - core
    place = ring_place(s, wide, deep)
    after = ring_owner((place + 1) % n_src, wide, deep)
    before = ring_owner((place + n_src - 1) % n_src, wide, deep)
    xb, width = x_own.shape
    yb = y_own.shape[0]
    rows, cols = n_tgt * xb, n_src * yb
    half = yb // 2
    part = half // CHUNKS
    scale = 1.0 / (width * EPSILON)

    barrier = pltpu.get_barrier_semaphore()
    for d in range(1, n_tgt):
        pl.semaphore_signal(
            barrier, inc=1, device_id={"tgt": (t + d) % n_tgt}, device_id_type=pl.DeviceIdType.MESH
        )

    def greet(d, carry):
        pl.semaphore_signal(
            barrier, inc=1, device_id={"src": (s + d) % n_src}, device_id_type=pl.DeviceIdType.MESH
        )
        return carry

    lax.fori_loop(1, n_src, greet, 0)
    pl.semaphore_wait(barrier, n_src + n_tgt - 2)

    def owner_of(k, way):
        return ring_owner((place + n_src + (k if way else -k)) % n_src, wide, deep)

    def ring_copy(k, way, c, first=False):
        offset = way * half + c * part
        sent = pl.multiple_of(owner_of(k - 1, way) * yb + offset, part)
        source = y_own.at[pl.ds(offset, part)] if first else y_all.at[pl.ds(sent, part)]
        return pltpu.make_async_remote_copy(
            src_ref=source,
            dst_ref=y_all.at[pl.ds(sent, part)],
            send_sem=ring_send.at[k, way, c],
            recv_sem=ring_recv.at[k, way, c],
            device_id={"src": before if way else after},
            device_id_type=pl.DeviceIdType.MESH,
        )

    def ring_arrival(k, way, c):
        offset = way * half + c * part
        got = pl.multiple_of(owner_of(k, way) * yb + offset, part)
        return pltpu.make_async_remote_copy(
            src_ref=y_all.at[pl.ds(got, part)],
            dst_ref=y_all.at[pl.ds(got, part)],
            send_sem=ring_send.at[k, way, c],
            recv_sem=ring_recv.at[k, way, c],
            device_id={"src": before if way else after},
            device_id_type=pl.DeviceIdType.MESH,
        )

    def x_copy(source, slot, send, recv, target):
        return pltpu.make_async_remote_copy(
            src_ref=source,
            dst_ref=x_all.at[slot],
            send_sem=send,
            recv_sem=recv,
            device_id={"tgt": target},
            device_id_type=pl.DeviceIdType.MESH,
        )

    order = [(way, c) for c in range(CHUNKS) for way in range(2)]
    for way, c in order:
        ring_copy(1, way, c, first=True).start()
    for d in range(1, n_y):
        target = ((y_me + d) % n_y) * 2 + core
        x_copy(x_own, t, y_send.at[d], y_recv.at[d], target).start()
    x_copy(x_own, t, core_send.at[0], core_recv.at[0], partner).start()

    a_col[...] = upright((log_tgt[...] + pot[...] / EPSILON) * LOG2E)
    row_top[...] = jnp.full_like(row_top, LOW)
    row_sum[...] = jnp.zeros_like(row_sum)

    def prepare_x(slot, values):
        where = pl.ds(pl.multiple_of(slot * xb, xb), xb)
        x_norm[where, :] = jnp.broadcast_to(jnp.sum(values * values, axis=1, keepdims=True), (xb, LANES))
        high, low = halves(values * (2.0 * scale * LOG2E))
        x_ops[where, 0:width] = high
        x_ops[where, width : 2 * width] = low
        x_ops[where, 2 * width : 3 * width] = high

    def prepare_y(first, values):
        where = pl.ds(first, half)
        norm = jnp.broadcast_to(jnp.sum(values * values, axis=1, keepdims=True), (half, LANES))
        y_norm[where, :] = norm
        a_col[where, :] = a_col[where, :] - norm * (scale * LOG2E)
        high, low = halves(values)
        y_ops[where, 0:width] = high
        y_ops[where, width : 2 * width] = high
        y_ops[where, 2 * width : 3 * width] = low

    prepare_x(t, x_own[...])
    for way in range(2):
        here = pl.multiple_of(s * yb + way * half, half)
        prepare_y(here, y_own[way * half : (way + 1) * half, :])

    def pass_on(k, carry):
        for way, c in order:
            ring_arrival(k, way, c).wait_recv()

            @pl.when(k < n_src - 1)
            def _():
                ring_copy(k + 1, way, c).start()

        for way in range(2):
            here = pl.multiple_of(owner_of(k, way) * yb + way * half, half)
            prepare_y(here, y_all[pl.ds(here, half), :])
        return carry

    lax.fori_loop(1, 3, pass_on, 0)

    for d in range(1, n_y):
        slot = ((y_me + n_y - d) % n_y) * 2 + core
        x_copy(x_all.at[slot], slot, y_send.at[d], y_recv.at[d], partner).wait_recv()
        x_copy(x_all.at[slot], slot, core_send.at[d], core_recv.at[d], partner).start()
        prepare_x(slot, x_all[slot])
    for d in range(n_y):
        slot = ((y_me + n_y - d) % n_y) * 2 + 1 - core
        x_copy(x_all.at[slot], slot, core_send.at[d], core_recv.at[d], partner).wait_recv()
        prepare_x(slot, x_all[slot])

    wide_rows = min(512, rows)

    def row_sweep(k, carry):
        for way in range(2):
            here = pl.ds(pl.multiple_of(owner_of(k, way) * yb + way * half, half), half)
            left = y_ops[here, :]
            bias = across(a_col[here, :], wide_rows)
            for first in range(0, rows, wide_rows):
                span = slice(first, first + wide_rows)
                scores = contract(left, x_ops[span, :]) + bias
                old = row_top[:, span]
                top = jnp.maximum(old, jnp.max(scores, axis=0, keepdims=True))
                total = jnp.sum(jnp.exp2(scores - top), axis=0, keepdims=True)
                row_sum[:, span] = row_sum[:, span] * jnp.exp2(old - top) + total
                row_top[:, span] = top
        return carry

    def turn(k, carry):
        pass_on(k, 0)
        lax.fori_loop(jnp.minimum(2 * (k - 3), k), jnp.minimum(2 * (k - 2), k + 1), row_sweep, 0)
        return carry

    lax.fori_loop(3, n_src, turn, 0)

    def row_copy(d, slot):
        return pltpu.make_async_remote_copy(
            src_ref=row_parts.at[slot],
            dst_ref=row_parts.at[slot],
            send_sem=row_send.at[d],
            recv_sem=row_recv.at[d],
            device_id={"tgt": (t + d) % n_tgt},
            device_id_type=pl.DeviceIdType.MESH,
        )

    row_parts[t] = row_top[...] + jnp.log2(row_sum[...])
    for d in range(1, n_tgt):
        row_copy(d, t).start()
    norms = flat(x_norm[...])
    for d in range(1, n_tgt):
        row_copy(d, (t + n_tgt - d) % n_tgt).wait_recv()
    lse = combine(row_parts, n_tgt)
    b_col[...] = upright(log_src[...] * LOG2E - lse)
    src_out[...] = norms / width - (EPSILON * LN2) * lse

    wide_cols = min(512, cols)

    def column_sweep(index, carry):
        span = pl.ds(pl.multiple_of(index * wide_cols, wide_cols), wide_cols)
        right = y_ops[span, :]
        top = jnp.full((1, wide_cols), LOW, jnp.float32)
        total = jnp.zeros((1, wide_cols), jnp.float32)
        for first in range(0, rows, wide_rows):
            here = slice(first, first + wide_rows)
            scores = contract(x_ops[here, :], right) + across(b_col[here, :], wide_cols)
            old = top
            top = jnp.maximum(old, jnp.max(scores, axis=0, keepdims=True))
            total = total * jnp.exp2(old - top) + jnp.sum(jnp.exp2(scores - top), axis=0, keepdims=True)
        col_parts[s, :, span] = top + jnp.log2(total)
        return carry

    lax.fori_loop(0, cols // wide_cols, column_sweep, 0)

    def col_copy(d, slot):
        return pltpu.make_async_remote_copy(
            src_ref=col_parts.at[slot],
            dst_ref=col_parts.at[slot],
            send_sem=col_send.at[d],
            recv_sem=col_recv.at[d],
            device_id={"src": (s + d) % n_src},
            device_id_type=pl.DeviceIdType.MESH,
        )

    def send_columns(d, carry):
        col_copy(d, s).start()
        return carry

    def take_columns(d, carry):
        col_copy(d, (s + n_src - d) % n_src).wait_recv()
        return carry

    lax.fori_loop(1, n_src, send_columns, 0)
    norms = flat(y_norm[...])
    lax.fori_loop(1, n_src, take_columns, 0)
    tgt_out[...] = norms / width - (EPSILON * LN2) * combine(col_parts, n_src)

    def settle_ring(k, carry):
        for way, c in order:
            ring_copy(k, way, c).wait_send()
        return carry

    def settle_columns(d, carry):
        col_copy(d, s).wait_send()
        return carry

    lax.fori_loop(1, n_src, settle_ring, 0)
    lax.fori_loop(1, n_src, settle_columns, 0)
    for d in range(1, n_y):
        x_copy(x_own, t, y_send.at[d], y_recv.at[d], partner).wait_send()
    for d in range(n_y):
        x_copy(x_own, t, core_send.at[d], core_recv.at[d], partner).wait_send()
    for d in range(1, n_tgt):
        row_copy(d, t).wait_send()


def shards(n_src, n_tgt, src_embed, tgt_embed, log_src, log_tgt, tgt_pot):
    xb, width = src_embed.shape
    yb = tgt_embed.shape[0]
    rows, cols = n_tgt * xb, n_src * yb
    wide = max(w for w in range(1, n_src + 1) if n_src % w == 0 and 2 * w * w <= n_src)
    deep = n_src // wide
    sem = pltpu.SemaphoreType.DMA
    vmem = pl.BlockSpec(memory_space=pltpu.VMEM)
    f32, bf16 = jnp.float32, jnp.bfloat16
    src_dual, tgt_dual = pl.pallas_call(
        functools.partial(kernel, n_src, n_tgt, wide, deep),
        out_shape=(jax.ShapeDtypeStruct((1, rows), f32), jax.ShapeDtypeStruct((1, cols), f32)),
        in_specs=[vmem] * 5,
        out_specs=(vmem, vmem),
        scratch_shapes=[
            pltpu.VMEM((n_tgt, xb, width), f32),
            pltpu.VMEM((cols, width), f32),
            pltpu.VMEM((rows, 3 * width), bf16),
            pltpu.VMEM((cols, 3 * width), bf16),
            pltpu.VMEM((cols, LANES), f32),
            pltpu.VMEM((rows, LANES), f32),
            pltpu.VMEM((rows, LANES), f32),
            pltpu.VMEM((cols, LANES), f32),
            pltpu.VMEM((1, rows), f32),
            pltpu.VMEM((1, rows), f32),
            pltpu.VMEM((n_tgt, 1, rows), f32),
            pltpu.VMEM((n_src, 1, cols), f32),
            sem((n_src, 2, CHUNKS)),
            sem((n_src, 2, CHUNKS)),
            sem((n_tgt // 2,)),
            sem((n_tgt // 2,)),
            sem((n_tgt // 2,)),
            sem((n_tgt // 2,)),
            sem((n_tgt,)),
            sem((n_tgt,)),
            sem((n_src,)),
            sem((n_src,)),
        ],
        compiler_params=pltpu.CompilerParams(
            collective_id=0, has_side_effects=True, vmem_limit_bytes=52 * 1024 * 1024
        ),
        cost_estimate=pl.CostEstimate(
            flops=12 * rows * cols * width,
            bytes_accessed=4 * (rows + cols) * width,
            transcendentals=2 * rows * cols,
        ),
    )(src_embed, tgt_embed, log_src[None, :], log_tgt[None, :], tgt_pot[None, :])
    return src_dual.reshape(rows), tgt_dual.reshape(cols)


def solution(mesh):
    in_specs = (P(("src", "tgt"), None), P(("tgt", "src"), None), P("src"), P("tgt"), P("tgt"))
    out_specs = (P("src"), P("tgt"))
    body = functools.partial(shards, mesh.shape["src"], mesh.shape["tgt"])
    return jax.shard_map(body, mesh=mesh, in_specs=in_specs, out_specs=out_specs, check_vma=False)
```

time: 279 us -> 82.9 us (0.30)
  waiting for transfers between devices: 101 us -> 0 us
  Pallas kernels: 0 us -> 76.4 us
  blocking collectives: 71.7 us -> 0 us
  other arithmetic: 49.5 us -> 0 us
  matrix products: 41.2 us -> 0 us
  between operations: 14.2 us -> 0.65 us
  local copies, waits for them, and re-layouts: 0.37 us -> 5.41 us
    all_gather x2 -> x0, waiting for transfers between devices: 99.8 us -> none  [the longest x1 73.6 us: shards(): targets = lax.all_gather(tgt_embed, 'src', axis=0, tiled=True)]
    pallas_call x0 -> x1, Pallas kernels: none -> 76.4 us  [shards(): pl.pallas_call(functools.partial(kernel, n_src, n_tgt, wide, deep), out_s...]
    all_gather x4 -> x0, blocking collectives: 71.7 us -> none  [combined_all(): everything = jax.tree.map(lambda part: lax.all_gather(part, axis), shard)]
    dot_general x1 -> x0, matrix products: 41.2 us -> none  [cross_inner(): lax.dot_general(left, right, (((1,), (1,)), ((), ())), precision=lax.Prec...]
    reduce_sum x4 -> x0, other arithmetic: 35 us -> none  [the longest x1 15.2 us: row_lse(): local_sum = jnp.sum(jnp.exp(scores - local_top[:, None]), axis=1)]
    reduce_max x1 -> x0, other arithmetic: 13.7 us -> none  [column_lse(): local_top = jnp.max(scores, axis=0)]
    unnamed x8 -> x12, local copies, waits for them, and re-layouts: 0.02 us -> 5.41 us
  transfers between devices with their start and end apart: 2 -> 0, of which waited for: 2 -> 0; matrix products, arithmetic and copies ran while one was open for 1% -> 0% of each run, Pallas kernels for 0% -> 0%
where the time goes in v1:
time: 82.9 us; the launch traced here: 82.5 us
  Pallas kernels  76.4 us (92%)
  local copies, waits for them, and re-layouts  5.41 us (7%)
    pallas_call x1, Pallas kernels, shards(): pl.pallas_call(functools.partial(kernel, n_src, n_tgt, wide, deep), out_s...  76.4 us
    unnamed x12, local copies, waits for them, and re-layouts  5.41 us

profile of v1, /device:TPU:0, one launch (start us, length us, event | category | flops | bytes accessed | tf_op | source)
XLA Modules:
  0.0 82.5 jit_solution(6373213577679566005)
XLA Ops:
  0.6 0.0 copy-start
  0.6 1.0 %copy-done = f32[512,256]{1,0:T(8,128)S(1)} copy-done((f32[512,256]{1,0:T(8,128)S(1)}, f32[512,256]{1,0:T(8,128)}, u32[]{:S(2)}) %copy-start) | copy-done | bytes 524312
  1.7 0.0 copy-start.1
  1.7 1.0 %copy-done.1 = f32[512,256]{1,0:T(8,128)S(1)} copy-done((f32[512,256]{1,0:T(8,128)S(1)}, f32[512,256]{1,0:T(8,128)}, u32[]{:S(2)}) %copy-start.1) | copy-done | bytes 524312
  2.7 0.0 copy-start.2
  2.7 0.7 copy-done.2
  3.4 0.0 copy-start.3
  3.4 0.7 copy-done.3
  4.2 0.0 copy-start.4
  4.2 0.7 copy-done.4
  4.8 76.4 %shard_map.68 = (f32[1,2048]{1,0:T(1,128)S(1)}, f32[1,4096]{1,0:T(1,128)S(1)}) custom-call(f32[512,256]{1,0:T(8,128)S(1)} %copy-done, f32[512,256]{1,0:T(8,128)S(1)} %copy-done.1, f32[1,2048]{1,0:T(1,128)S(1)} %bitcast.9, f32[1,4096]{1,0:T(1,128)S(1)} %bitcast.7, f32[1,4096]{1,0:T(1,128)S(1)} %bitcast.8), custom_call_target="tpu_custom_call" | custom-call | flops 25769803776 | bytes 6291456 | tf_op jit(solution)/shard_map/pallas_call | solution.py:309
  81.3 0.6 copy.9
  81.9 0.6 copy.10
Async XLA Ops:
  0.6 1.0 %copy-start = (f32[512,256]{1,0:T(8,128)S(1)}, f32[512,256]{1,0:T(8,128)}, u32[]{:S(2)}) copy-start(f32[512,256]{1,0:T(8,128)} %x_own.1) | copy-start | bytes 1572868
  1.7 1.0 %copy-start.1 = (f32[512,256]{1,0:T(8,128)S(1)}, f32[512,256]{1,0:T(8,128)}, u32[]{:S(2)}) copy-start(f32[512,256]{1,0:T(8,128)} %y_own.1) | copy-start | bytes 1572868
  2.7 0.7 copy-start.2
  3.4 0.7 copy-start.3
  4.2 0.7 copy-start.4

commit v2 on v1

--- a/solution.py
+++ b/solution.py
@@ -59,11 +59,11 @@
 
 def kernel(
     n_src, n_tgt, wide, deep,
-    x_own, y_own, log_src, log_tgt, pot, src_out, tgt_out,
-    x_all, y_all, x_ops, y_ops, a_col, b_col, x_norm, y_norm,
-    row_top, row_sum, row_parts, col_parts,
+    x_own, y_own, log_src_in, log_tgt_in, pot_in, src_out, tgt_out,
+    x_all, y_all, x_ops, products, a_col, b_rows, x_norm, y_norm,
+    log_src, log_tgt, pot, row_top, row_sum, row_parts, col_parts,
     ring_send, ring_recv, y_send, y_recv, core_send, core_recv,
-    row_send, row_recv, col_send, col_recv,
+    row_send, row_recv, col_send, col_recv, local,
 ):
     s = lax.axis_index("src")
     t = lax.axis_index("tgt")
@@ -80,6 +80,17 @@
     part = half // CHUNKS
     scale = 1.0 / (width * EPSILON)
 
+    own_rows = pl.ds(pl.multiple_of(s * yb, yb), yb)
+    own = [
+        pltpu.make_async_copy(log_tgt_in, log_tgt, local.at[0]),
+        pltpu.make_async_copy(pot_in, pot, local.at[1]),
+        pltpu.make_async_copy(x_own, x_all.at[t], local.at[2]),
+        pltpu.make_async_copy(y_own, y_all.at[own_rows], local.at[3]),
+        pltpu.make_async_copy(log_src_in, log_src, local.at[4]),
+    ]
+    for copy in own:
+        copy.start()
+
     barrier = pltpu.get_barrier_semaphore()
     for d in range(1, n_tgt):
         pl.semaphore_signal(
@@ -141,6 +152,8 @@
         x_copy(x_own, t, y_send.at[d], y_recv.at[d], target).start()
     x_copy(x_own, t, core_send.at[0], core_recv.at[0], partner).start()
 
+    for copy in own:
+        copy.wait()
     a_col[...] = upright((log_tgt[...] + pot[...] / EPSILON) * LOG2E)
     row_top[...] = jnp.full_like(row_top, LOW)
     row_sum[...] = jnp.zeros_like(row_sum)
@@ -153,35 +166,22 @@
         x_ops[where, width : 2 * width] = low
         x_ops[where, 2 * width : 3 * width] = high
 
-    def prepare_y(first, values):
-        where = pl.ds(first, half)
-        norm = jnp.broadcast_to(jnp.sum(values * values, axis=1, keepdims=True), (half, LANES))
-        y_norm[where, :] = norm
-        a_col[where, :] = a_col[where, :] - norm * (scale * LOG2E)
-        high, low = halves(values)
-        y_ops[where, 0:width] = high
-        y_ops[where, width : 2 * width] = high
-        y_ops[where, 2 * width : 3 * width] = low
-
-    prepare_x(t, x_own[...])
-    for way in range(2):
-        here = pl.multiple_of(s * yb + way * half, half)
-        prepare_y(here, y_own[way * half : (way + 1) * half, :])
-
-    def pass_on(k, carry):
-        for way, c in order:
+    prepare_x(t, x_all[t])
+
+    def pass_on(k, c):
+        for way in range(2):
             ring_arrival(k, way, c).wait_recv()
 
             @pl.when(k < n_src - 1)
             def _():
                 ring_copy(k + 1, way, c).start()
 
-        for way in range(2):
-            here = pl.multiple_of(owner_of(k, way) * yb + way * half, half)
-            prepare_y(here, y_all[pl.ds(here, half), :])
-        return carry
-
-    lax.fori_loop(1, 3, pass_on, 0)
+    def first_turns(k, carry):
+        for c in range(CHUNKS):
+            pass_on(k, c)
+        return carry
+
+    lax.fori_loop(1, 3, first_turns, 0)
 
     for d in range(1, n_y):
         slot = ((y_me + n_y - d) % n_y) * 2 + core
@@ -198,11 +198,17 @@
     def row_sweep(k, carry):
         for way in range(2):
             here = pl.ds(pl.multiple_of(owner_of(k, way) * yb + way * half, half), half)
-            left = y_ops[here, :]
-            bias = across(a_col[here, :], wide_rows)
+            values = y_all[here, :]
+            norm = jnp.broadcast_to(jnp.sum(values * values, axis=1, keepdims=True), (half, LANES))
+            y_norm[here, :] = norm
+            bias = across(a_col[here, :] - norm * (scale * LOG2E), wide_rows)
+            high, low = halves(values)
+            left = jnp.concatenate([high, high, low], axis=1)
             for first in range(0, rows, wide_rows):
                 span = slice(first, first + wide_rows)
-                scores = contract(left, x_ops[span, :]) + bias
+                product = contract(left, x_ops[span, :])
+                products[here, span] = product
+                scores = product + bias
                 old = row_top[:, span]
                 top = jnp.maximum(old, jnp.max(scores, axis=0, keepdims=True))
                 total = jnp.sum(jnp.exp2(scores - top), axis=0, keepdims=True)
@@ -212,7 +218,11 @@
 
     def turn(k, carry):
         pass_on(k, 0)
-        lax.fori_loop(jnp.minimum(2 * (k - 3), k), jnp.minimum(2 * (k - 2), k + 1), row_sweep, 0)
+        done = jnp.minimum(2 * (k - 3), k)
+        ready = jnp.minimum(2 * (k - 3) + 1, k)
+        lax.fori_loop(done, ready, row_sweep, 0)
+        pass_on(k, 1)
+        lax.fori_loop(ready, jnp.minimum(2 * (k - 2), k + 1), row_sweep, 0)
         return carry
 
     lax.fori_loop(3, n_src, turn, 0)
@@ -234,26 +244,31 @@
     for d in range(1, n_tgt):
         row_copy(d, (t + n_tgt - d) % n_tgt).wait_recv()
     lse = combine(row_parts, n_tgt)
-    b_col[...] = upright(log_src[...] * LOG2E - lse)
+    b_rows[...] = jnp.broadcast_to(log_src[...] * LOG2E - lse, b_rows.shape)
     src_out[...] = norms / width - (EPSILON * LN2) * lse
 
-    wide_cols = min(512, cols)
+    group = min(256, cols)
 
     def column_sweep(index, carry):
-        span = pl.ds(pl.multiple_of(index * wide_cols, wide_cols), wide_cols)
-        right = y_ops[span, :]
-        top = jnp.full((1, wide_cols), LOW, jnp.float32)
-        total = jnp.zeros((1, wide_cols), jnp.float32)
-        for first in range(0, rows, wide_rows):
-            here = slice(first, first + wide_rows)
-            scores = contract(x_ops[here, :], right) + across(b_col[here, :], wide_cols)
-            old = top
-            top = jnp.maximum(old, jnp.max(scores, axis=0, keepdims=True))
-            total = total * jnp.exp2(old - top) + jnp.sum(jnp.exp2(scores - top), axis=0, keepdims=True)
-        col_parts[s, :, span] = top + jnp.log2(total)
-        return carry
-
-    lax.fori_loop(0, cols // wide_cols, column_sweep, 0)
+        begin = pl.multiple_of(index * group, group)
+        tops, totals = [], []
+        for first in range(0, group, 8):
+            here = pl.ds(pl.multiple_of(begin + first, 8), 8)
+            scores = [
+                products[here, at : at + LANES] + b_rows[:, at : at + LANES]
+                for at in range(0, rows, LANES)
+            ]
+            top = functools.reduce(jnp.maximum, scores)
+            tops.append(top)
+            totals.append(sum(jnp.exp2(score - top) for score in scores))
+        lane_top = jnp.transpose(jnp.concatenate(tops, axis=0))
+        lane_total = jnp.transpose(jnp.concatenate(totals, axis=0))
+        top = jnp.max(lane_top, axis=0, keepdims=True)
+        total = jnp.sum(lane_total * jnp.exp2(lane_top - top), axis=0, keepdims=True)
+        col_parts[s, :, pl.ds(begin, group)] = top + jnp.log2(total)
+        return carry
+
+    lax.fori_loop(0, cols // group, column_sweep, 0)
 
     def col_copy(d, slot):
         return pltpu.make_async_remote_copy(
@@ -290,9 +305,9 @@
     lax.fori_loop(1, n_src, settle_ring, 0)
     lax.fori_loop(1, n_src, settle_columns, 0)
     for d in range(1, n_y):
-        x_copy(x_own, t, y_send.at[d], y_recv.at[d], partner).wait_send()
+        x_copy(x_all.at[t], t, y_send.at[d], y_recv.at[d], partner).wait_send()
     for d in range(n_y):
-        x_copy(x_own, t, core_send.at[d], core_recv.at[d], partner).wait_send()
+        x_copy(x_all.at[t], t, core_send.at[d], core_recv.at[d], partner).wait_send()
     for d in range(1, n_tgt):
         row_copy(d, t).wait_send()
 
@@ -309,17 +324,20 @@
     src_dual, tgt_dual = pl.pallas_call(
         functools.partial(kernel, n_src, n_tgt, wide, deep),
         out_shape=(jax.ShapeDtypeStruct((1, rows), f32), jax.ShapeDtypeStruct((1, cols), f32)),
-        in_specs=[vmem] * 5,
+        in_specs=[pl.BlockSpec(memory_space=pl.ANY)] * 5,
         out_specs=(vmem, vmem),
         scratch_shapes=[
             pltpu.VMEM((n_tgt, xb, width), f32),
             pltpu.VMEM((cols, width), f32),
             pltpu.VMEM((rows, 3 * width), bf16),
-            pltpu.VMEM((cols, 3 * width), bf16),
+            pltpu.VMEM((cols, rows), f32),
             pltpu.VMEM((cols, LANES), f32),
-            pltpu.VMEM((rows, LANES), f32),
+            pltpu.VMEM((8, rows), f32),
             pltpu.VMEM((rows, LANES), f32),
             pltpu.VMEM((cols, LANES), f32),
+            pltpu.VMEM((1, rows), f32),
+            pltpu.VMEM((1, cols), f32),
+            pltpu.VMEM((1, cols), f32),
             pltpu.VMEM((1, rows), f32),
             pltpu.VMEM((1, rows), f32),
             pltpu.VMEM((n_tgt, 1, rows), f32),
@@ -334,12 +352,13 @@
             sem((n_tgt,)),
             sem((n_src,)),
             sem((n_src,)),
+            sem((5,)),
         ],
         compiler_params=pltpu.CompilerParams(
-            collective_id=0, has_side_effects=True, vmem_limit_bytes=52 * 1024 * 1024
+            collective_id=0, has_side_effects=True, vmem_limit_bytes=60 * 1024 * 1024
         ),
         cost_estimate=pl.CostEstimate(
-            flops=12 * rows * cols * width,
+            flops=6 * rows * cols * width,
             bytes_accessed=4 * (rows + cols) * width,
             transcendentals=2 * rows * cols,
         ),

time: 82.9 us -> 70 us (0.84)
  Pallas kernels: 76.4 us -> 67.2 us
  local copies, waits for them, and re-layouts: 5.41 us -> 1.91 us
    pallas_call x1, Pallas kernels: 76.4 us -> 67.2 us  [shards(): pl.pallas_call(functools.partial(kernel, n_src, n_tgt, wide, deep), out_s...]
    unnamed x12 -> x4, local copies, waits for them, and re-layouts: 5.41 us -> 1.91 us
where the time goes in v2:
time: 70 us; the launch traced here: 69.8 us
  Pallas kernels  67.2 us (96%)
  local copies, waits for them, and re-layouts  1.91 us (3%)
    pallas_call x1, Pallas kernels, shards(): pl.pallas_call(functools.partial(kernel, n_src, n_tgt, wide, deep), out_s...  67.2 us
    unnamed x4, local copies, waits for them, and re-layouts  1.91 us

profile of v2, /device:TPU:0, one launch (start us, length us, event | category | flops | bytes accessed | tf_op | source)
XLA Modules:
  0.0 69.8 jit_solution(18407292694061154866)
XLA Ops:
  0.6 67.2 %shard_map.68 = (f32[1,2048]{1,0:T(1,128)}, f32[1,4096]{1,0:T(1,128)}) custom-call(f32[512,256]{1,0:T(8,128)} %x_own.1, f32[512,256]{1,0:T(8,128)} %y_own.1, f32[1,2048]{1,0:T(1,128)} %bitcast.9, f32[1,4096]{1,0:T(1,128)} %bitcast.7, f32[1,4096]{1,0:T(1,128)} %bitcast.8), custom_call_target="tpu_custom_call" | custom-call | flops 12884901888 | bytes 6291456 | tf_op jit(solution)/shard_map/pallas_call | solution.py:324
  67.9 0.0 copy-start
  67.9 1.3 %copy.9 = f32[2048]{0:T(1024)} copy(f32[2048]{0:T(1024)} %bitcast.6) | data formatting | bytes 16384
  69.2 0.0 copy-done
  69.2 0.6 copy.10
Async XLA Ops:
  67.9 1.3 %copy-start = (f32[1,4096]{1,0:T(1,128)S(1)}, f32[1,4096]{1,0:T(1,128)}, u32[]{:S(2)}) copy-start(f32[1,4096]{1,0:T(1,128)} %get-tuple-element.5) | copy-start | bytes 49156

commit v3 on v2

--- a/solution.py
+++ b/solution.py
@@ -13,7 +13,8 @@
 LN2 = math.log(2.0)
 LOW = -1e38
 LANES = 128
-CHUNKS = 2
+CHUNKS = 4
+PARTS = 2
 
 
 def ring_place(src, wide, deep):
@@ -107,7 +108,7 @@
     pl.semaphore_wait(barrier, n_src + n_tgt - 2)
 
     def owner_of(k, way):
-        return ring_owner((place + n_src + (k if way else -k)) % n_src, wide, deep)
+        return ring_owner((place + n_src + (2 * way - 1) * k) % n_src, wide, deep)
 
     def ring_copy(k, way, c, first=False):
         offset = way * half + c * part
@@ -173,7 +174,7 @@
             ring_arrival(k, way, c).wait_recv()
 
             @pl.when(k < n_src - 1)
-            def _():
+            def _(way=way):
                 ring_copy(k + 1, way, c).start()
 
     def first_turns(k, carry):
@@ -195,37 +196,49 @@
 
     wide_rows = min(512, rows)
 
-    def row_sweep(k, carry):
-        for way in range(2):
-            here = pl.ds(pl.multiple_of(owner_of(k, way) * yb + way * half, half), half)
-            values = y_all[here, :]
-            norm = jnp.broadcast_to(jnp.sum(values * values, axis=1, keepdims=True), (half, LANES))
-            y_norm[here, :] = norm
-            bias = across(a_col[here, :] - norm * (scale * LOG2E), wide_rows)
-            high, low = halves(values)
-            left = jnp.concatenate([high, high, low], axis=1)
-            for first in range(0, rows, wide_rows):
-                span = slice(first, first + wide_rows)
-                product = contract(left, x_ops[span, :])
-                products[here, span] = product
-                scores = product + bias
-                old = row_top[:, span]
-                top = jnp.maximum(old, jnp.max(scores, axis=0, keepdims=True))
-                total = jnp.sum(jnp.exp2(scores - top), axis=0, keepdims=True)
-                row_sum[:, span] = row_sum[:, span] * jnp.exp2(old - top) + total
-                row_top[:, span] = top
+    def row_sweep(first, count):
+        here = pl.ds(first, count)
+        values = y_all[here, :]
+        norm = jnp.broadcast_to(jnp.sum(values * values, axis=1, keepdims=True), (count, LANES))
+        y_norm[here, :] = norm
+        bias = across(a_col[here, :] - norm * (scale * LOG2E), wide_rows)
+        high, low = halves(values)
+        left = jnp.concatenate([high, high, low], axis=1)
+        for begin in range(0, rows, wide_rows):
+            span = slice(begin, begin + wide_rows)
+            product = contract(left, x_ops[span, :])
+            products[here, span] = product
+            scores = product + bias
+            old = row_top[:, span]
+            top = jnp.maximum(old, jnp.max(scores, axis=0, keepdims=True))
+            total = jnp.sum(jnp.exp2(scores - top), axis=0, keepdims=True)
+            row_sum[:, span] = row_sum[:, span] * jnp.exp2(old - top) + total
+            row_top[:, span] = top
+
+    def half_sweep(unit, carry):
+        k, way = unit // 2, unit % 2
+        row_sweep(pl.multiple_of(owner_of(k, way) * yb + way * half, half), half)
         return carry
 
     def turn(k, carry):
-        pass_on(k, 0)
-        done = jnp.minimum(2 * (k - 3), k)
-        ready = jnp.minimum(2 * (k - 3) + 1, k)
-        lax.fori_loop(done, ready, row_sweep, 0)
-        pass_on(k, 1)
-        lax.fori_loop(ready, jnp.minimum(2 * (k - 2), k + 1), row_sweep, 0)
-        return carry
-
-    lax.fori_loop(3, n_src, turn, 0)
+        done = jnp.minimum(CHUNKS * (k - 3), 2 * k)
+        for c in range(CHUNKS):
+            pass_on(k, c)
+            whole = 2 if c == CHUNKS - 1 else 0
+            ready = jnp.minimum(CHUNKS * (k - 3) + c + 1, 2 * k + whole)
+            lax.fori_loop(done, ready, half_sweep, 0)
+            done = ready
+        return carry
+
+    lax.fori_loop(3, n_src - 1, turn, 0)
+    last = n_src - 1
+    quarter = half // 2
+    for c in range(CHUNKS):
+        pass_on(last, c)
+        if c % 2 == 1:
+            for way in range(2):
+                first = owner_of(last, way) * yb + way * half + (c // 2) * quarter
+                row_sweep(pl.multiple_of(first, quarter), quarter)
 
     def row_copy(d, slot):
         return pltpu.make_async_remote_copy(
@@ -247,7 +260,7 @@
     b_rows[...] = jnp.broadcast_to(log_src[...] * LOG2E - lse, b_rows.shape)
     src_out[...] = norms / width - (EPSILON * LN2) * lse
 
-    group = min(256, cols)
+    group = min(256, cols // PARTS)
 
     def column_sweep(index, carry):
         begin = pl.multiple_of(index * group, group)
@@ -268,27 +281,33 @@
         col_parts[s, :, pl.ds(begin, group)] = top + jnp.log2(total)
         return carry
 
-    lax.fori_loop(0, cols // group, column_sweep, 0)
-
-    def col_copy(d, slot):
-        return pltpu.make_async_remote_copy(
-            src_ref=col_parts.at[slot],
-            dst_ref=col_parts.at[slot],
-            send_sem=col_send.at[d],
-            recv_sem=col_recv.at[d],
+    share = cols // PARTS
+
+    def col_copy(d, slot, h):
+        span = pl.ds(h * share, share)
+        return pltpu.make_async_remote_copy(
+            src_ref=col_parts.at[slot, :, span],
+            dst_ref=col_parts.at[slot, :, span],
+            send_sem=col_send.at[d, h],
+            recv_sem=col_recv.at[d, h],
             device_id={"src": (s + d) % n_src},
             device_id_type=pl.DeviceIdType.MESH,
         )
 
-    def send_columns(d, carry):
-        col_copy(d, s).start()
-        return carry
+    for h in range(PARTS):
+        lax.fori_loop(h * share // group, (h + 1) * share // group, column_sweep, 0)
+
+        def send_columns(d, carry, h=h):
+            col_copy(d, s, h).start()
+            return carry
+
+        lax.fori_loop(1, n_src, send_columns, 0)
 
     def take_columns(d, carry):
-        col_copy(d, (s + n_src - d) % n_src).wait_recv()
-        return carry
-
-    lax.fori_loop(1, n_src, send_columns, 0)
+        for h in range(PARTS):
+            col_copy(d, (s + n_src - d) % n_src, h).wait_recv()
+        return carry
+
     norms = flat(y_norm[...])
     lax.fori_loop(1, n_src, take_columns, 0)
     tgt_out[...] = norms / width - (EPSILON * LN2) * combine(col_parts, n_src)
@@ -299,7 +318,8 @@
         return carry
 
     def settle_columns(d, carry):
-        col_copy(d, s).wait_send()
+        for h in range(PARTS):
+            col_copy(d, s, h).wait_send()
         return carry
 
     lax.fori_loop(1, n_src, settle_ring, 0)
@@ -350,8 +370,8 @@
             sem((n_tgt // 2,)),
             sem((n_tgt,)),
             sem((n_tgt,)),
-            sem((n_src,)),
-            sem((n_src,)),
+            sem((n_src, PARTS)),
+            sem((n_src, PARTS)),
             sem((5,)),
         ],
         compiler_params=pltpu.CompilerParams(

time: 70 us -> 70 us (level)
  no operation moved by 1% of the time
where the time goes in v3:
time: 70 us; the launch traced here: 69.9 us
  Pallas kernels  67.3 us (96%)
  local copies, waits for them, and re-layouts  1.91 us (3%)
    pallas_call x1, Pallas kernels, shards(): pl.pallas_call(functools.partial(kernel, n_src, n_tgt, wide, deep), out_s...  67.3 us
    unnamed x4, local copies, waits for them, and re-layouts  1.91 us

profile of v3, /device:TPU:0, one launch (start us, length us, event | category | flops | bytes accessed | tf_op | source)
XLA Modules:
  0.0 69.9 jit_solution(10539934740207452100)
XLA Ops:
  0.6 67.3 %shard_map.68 = (f32[1,2048]{1,0:T(1,128)}, f32[1,4096]{1,0:T(1,128)}) custom-call(f32[512,256]{1,0:T(8,128)} %x_own.1, f32[512,256]{1,0:T(8,128)} %y_own.1, f32[1,2048]{1,0:T(1,128)} %bitcast.9, f32[1,4096]{1,0:T(1,128)} %bitcast.7, f32[1,4096]{1,0:T(1,128)} %bitcast.8), custom_call_target="tpu_custom_call" | custom-call | flops 12884901888 | bytes 6291456 | tf_op jit(solution)/shard_map/pallas_call | solution.py:344
  67.9 0.0 copy-start
  67.9 1.3 %copy.9 = f32[2048]{0:T(1024)} copy(f32[2048]{0:T(1024)} %bitcast.6) | data formatting | bytes 16384
  69.2 0.0 copy-done
  69.2 0.6 copy.10
Async XLA Ops:
  67.9 1.3 %copy-start = (f32[1,4096]{1,0:T(1,128)S(1)}, f32[1,4096]{1,0:T(1,128)}, u32[]{:S(2)}) copy-start(f32[1,4096]{1,0:T(1,128)} %get-tuple-element.5) | copy-start | bytes 49156

commit v4 on v3

--- a/solution.py
+++ b/solution.py
@@ -1,5 +1,4 @@
 import functools
-import math
 
 import jax
 import jax.numpy as jnp
@@ -9,8 +8,6 @@
 from jax.sharding import PartitionSpec as P
 
 EPSILON = 0.05
-LOG2E = math.log2(math.e)
-LN2 = math.log(2.0)
 LOW = -1e38
 LANES = 128
 CHUNKS = 4
@@ -54,8 +51,8 @@
 
 def combine(parts, count):
     top = functools.reduce(jnp.maximum, [parts[k] for k in range(count)])
-    total = sum(jnp.exp2(parts[k] - top) for k in range(count))
-    return top + jnp.log2(total)
+    total = sum(jnp.exp(parts[k] - top) for k in range(count))
+    return top + jnp.log(total)
 
 
 def kernel(
@@ -155,20 +152,49 @@
 
     for copy in own:
         copy.wait()
-    a_col[...] = upright((log_tgt[...] + pot[...] / EPSILON) * LOG2E)
+    a_col[...] = upright(log_tgt[...] + pot[...] / EPSILON)
     row_top[...] = jnp.full_like(row_top, LOW)
     row_sum[...] = jnp.zeros_like(row_sum)
 
     def prepare_x(slot, values):
         where = pl.ds(pl.multiple_of(slot * xb, xb), xb)
         x_norm[where, :] = jnp.broadcast_to(jnp.sum(values * values, axis=1, keepdims=True), (xb, LANES))
-        high, low = halves(values * (2.0 * scale * LOG2E))
+        high, low = halves(values * (2.0 * scale))
         x_ops[where, 0:width] = high
         x_ops[where, width : 2 * width] = low
         x_ops[where, 2 * width : 3 * width] = high
 
     prepare_x(t, x_all[t])
 
+    near = [t, partner]
+    far = [((y_me + d) % n_y) * 2 + c for d in range(1, n_y) for c in range(2)]
+
+    def row_sweep(first, count, slots):
+        here = pl.ds(first, count)
+        values = y_all[here, :]
+        norm = jnp.broadcast_to(jnp.sum(values * values, axis=1, keepdims=True), (count, LANES))
+        y_norm[here, :] = norm
+        bias = across(a_col[here, :] - norm * scale, xb)
+        high, low = halves(values)
+        left = jnp.concatenate([high, high, low], axis=1)
+        for slot in slots:
+            span = pl.ds(pl.multiple_of(slot * xb, xb), xb)
+            product = contract(left, x_ops[span, :])
+            products[here, span] = product
+            scores = product + bias
+            old = row_top[:, span]
+            top = jnp.maximum(old, jnp.max(scores, axis=0, keepdims=True))
+            total = jnp.sum(jnp.exp(scores - top), axis=0, keepdims=True)
+            row_sum[:, span] = row_sum[:, span] * jnp.exp(old - top) + total
+            row_top[:, span] = top
+
+    def half_first(k, way):
+        return pl.multiple_of(owner_of(k, way) * yb + way * half, half)
+
+    def early_sweep(unit, carry):
+        row_sweep(half_first(unit // 2, unit % 2), half, near)
+        return carry
+
     def pass_on(k, c):
         for way in range(2):
             ring_arrival(k, way, c).wait_recv()
@@ -178,46 +204,37 @@
                 ring_copy(k + 1, way, c).start()
 
     def first_turns(k, carry):
+        lax.fori_loop(2 * (k - 1), 2 * k, early_sweep, 0)
         for c in range(CHUNKS):
             pass_on(k, c)
         return carry
 
+    x_copy(x_all.at[partner], partner, core_send.at[0], core_recv.at[0], partner).wait_recv()
+    prepare_x(partner, x_all[partner])
     lax.fori_loop(1, 3, first_turns, 0)
+    lax.fori_loop(4, 6, early_sweep, 0)
 
     for d in range(1, n_y):
         slot = ((y_me + n_y - d) % n_y) * 2 + core
         x_copy(x_all.at[slot], slot, y_send.at[d], y_recv.at[d], partner).wait_recv()
         x_copy(x_all.at[slot], slot, core_send.at[d], core_recv.at[d], partner).start()
         prepare_x(slot, x_all[slot])
-    for d in range(n_y):
+    for d in range(1, n_y):
         slot = ((y_me + n_y - d) % n_y) * 2 + 1 - core
         x_copy(x_all.at[slot], slot, core_send.at[d], core_recv.at[d], partner).wait_recv()
         prepare_x(slot, x_all[slot])
 
-    wide_rows = min(512, rows)
-
-    def row_sweep(first, count):
-        here = pl.ds(first, count)
-        values = y_all[here, :]
-        norm = jnp.broadcast_to(jnp.sum(values * values, axis=1, keepdims=True), (count, LANES))
-        y_norm[here, :] = norm
-        bias = across(a_col[here, :] - norm * (scale * LOG2E), wide_rows)
-        high, low = halves(values)
-        left = jnp.concatenate([high, high, low], axis=1)
-        for begin in range(0, rows, wide_rows):
-            span = slice(begin, begin + wide_rows)
-            product = contract(left, x_ops[span, :])
-            products[here, span] = product
-            scores = product + bias
-            old = row_top[:, span]
-            top = jnp.maximum(old, jnp.max(scores, axis=0, keepdims=True))
-            total = jnp.sum(jnp.exp2(scores - top), axis=0, keepdims=True)
-            row_sum[:, span] = row_sum[:, span] * jnp.exp2(old - top) + total
-            row_top[:, span] = top
-
     def half_sweep(unit, carry):
         k, way = unit // 2, unit % 2
-        row_sweep(pl.multiple_of(owner_of(k, way) * yb + way * half, half), half)
+
+        @pl.when(k < 3)
+        def _():
+            row_sweep(half_first(k, way), half, far)
+
+        @pl.when(k >= 3)
+        def _():
+            row_sweep(half_first(k, way), half, near + far)
+
         return carry
 
     def turn(k, carry):
@@ -238,7 +255,7 @@
         if c % 2 == 1:
             for way in range(2):
                 first = owner_of(last, way) * yb + way * half + (c // 2) * quarter
-                row_sweep(pl.multiple_of(first, quarter), quarter)
+                row_sweep(pl.multiple_of(first, quarter), quarter, near + far)
 
     def row_copy(d, slot):
         return pltpu.make_async_remote_copy(
@@ -250,15 +267,15 @@
             device_id_type=pl.DeviceIdType.MESH,
         )
 
-    row_parts[t] = row_top[...] + jnp.log2(row_sum[...])
+    row_parts[t] = row_top[...] + jnp.log(row_sum[...])
     for d in range(1, n_tgt):
         row_copy(d, t).start()
     norms = flat(x_norm[...])
     for d in range(1, n_tgt):
         row_copy(d, (t + n_tgt - d) % n_tgt).wait_recv()
     lse = combine(row_parts, n_tgt)
-    b_rows[...] = jnp.broadcast_to(log_src[...] * LOG2E - lse, b_rows.shape)
-    src_out[...] = norms / width - (EPSILON * LN2) * lse
+    b_rows[...] = jnp.broadcast_to(log_src[...] - lse, b_rows.shape)
+    src_out[...] = norms / width - EPSILON * lse
 
     group = min(256, cols // PARTS)
 
@@ -273,12 +290,12 @@
             ]
             top = functools.reduce(jnp.maximum, scores)
             tops.append(top)
-            totals.append(sum(jnp.exp2(score - top) for score in scores))
+            totals.append(sum(jnp.exp(score - top) for score in scores))
         lane_top = jnp.transpose(jnp.concatenate(tops, axis=0))
         lane_total = jnp.transpose(jnp.concatenate(totals, axis=0))
         top = jnp.max(lane_top, axis=0, keepdims=True)
-        total = jnp.sum(lane_total * jnp.exp2(lane_top - top), axis=0, keepdims=True)
-        col_parts[s, :, pl.ds(begin, group)] = top + jnp.log2(total)
+        total = jnp.sum(lane_total * jnp.exp(lane_top - top), axis=0, keepdims=True)
+        col_parts[s, :, pl.ds(begin, group)] = top + jnp.log(total)
         return carry
 
     share = cols // PARTS
@@ -310,7 +327,7 @@
 
     norms = flat(y_norm[...])
     lax.fori_loop(1, n_src, take_columns, 0)
-    tgt_out[...] = norms / width - (EPSILON * LN2) * combine(col_parts, n_src)
+    tgt_out[...] = norms / width - EPSILON * combine(col_parts, n_src)
 
     def settle_ring(k, carry):
         for way, c in order:

time: 70 us -> 70.5 us (level)
  no operation moved by 1% of the time
where the time goes in v4:
time: 70.5 us; the launch traced here: 70.4 us
  Pallas kernels  67.8 us (96%)
  local copies, waits for them, and re-layouts  1.91 us (3%)
    pallas_call x1, Pallas kernels, shards(): pl.pallas_call(functools.partial(kernel, n_src, n_tgt, wide, deep), out_s...  67.8 us
    unnamed x4, local copies, waits for them, and re-layouts  1.91 us

profile of v4, /device:TPU:0, one launch (start us, length us, event | category | flops | bytes accessed | tf_op | source)
XLA Modules:
  0.0 70.4 jit_solution(10624697634900542446)
XLA Ops:
  0.6 67.8 %shard_map.68 = (f32[1,2048]{1,0:T(1,128)}, f32[1,4096]{1,0:T(1,128)}) custom-call(f32[512,256]{1,0:T(8,128)} %x_own.1, f32[512,256]{1,0:T(8,128)} %y_own.1, f32[1,2048]{1,0:T(1,128)} %bitcast.9, f32[1,4096]{1,0:T(1,128)} %bitcast.7, f32[1,4096]{1,0:T(1,128)} %bitcast.8), custom_call_target="tpu_custom_call" | custom-call | flops 12884901888 | bytes 6291456 | tf_op jit(solution)/shard_map/pallas_call | solution.py:361
  68.4 0.0 copy-start
  68.5 1.3 %copy.9 = f32[2048]{0:T(1024)} copy(f32[2048]{0:T(1024)} %bitcast.6) | data formatting | bytes 16384
  69.8 0.0 copy-done
  69.8 0.6 copy.10
Async XLA Ops:
  68.4 1.3 %copy-start = (f32[1,4096]{1,0:T(1,128)S(1)}, f32[1,4096]{1,0:T(1,128)}, u32[]{:S(2)}) copy-start(f32[1,4096]{1,0:T(1,128)} %get-tuple-element.5) | copy-start | bytes 49156

commit v5 on v3

--- a/solution.py
+++ b/solution.py
@@ -1,5 +1,4 @@
 import functools
-import math
 
 import jax
 import jax.numpy as jnp
@@ -9,8 +8,6 @@
 from jax.sharding import PartitionSpec as P
 
 EPSILON = 0.05
-LOG2E = math.log2(math.e)
-LN2 = math.log(2.0)
 LOW = -1e38
 LANES = 128
 CHUNKS = 4
@@ -54,8 +51,8 @@
 
 def combine(parts, count):
     top = functools.reduce(jnp.maximum, [parts[k] for k in range(count)])
-    total = sum(jnp.exp2(parts[k] - top) for k in range(count))
-    return top + jnp.log2(total)
+    total = sum(jnp.exp(parts[k] - top) for k in range(count))
+    return top + jnp.log(total)
 
 
 def kernel(
@@ -155,14 +152,14 @@
 
     for copy in own:
         copy.wait()
-    a_col[...] = upright((log_tgt[...] + pot[...] / EPSILON) * LOG2E)
+    a_col[...] = upright((log_tgt[...] + pot[...] / EPSILON))
     row_top[...] = jnp.full_like(row_top, LOW)
     row_sum[...] = jnp.zeros_like(row_sum)
 
     def prepare_x(slot, values):
         where = pl.ds(pl.multiple_of(slot * xb, xb), xb)
         x_norm[where, :] = jnp.broadcast_to(jnp.sum(values * values, axis=1, keepdims=True), (xb, LANES))
-        high, low = halves(values * (2.0 * scale * LOG2E))
+        high, low = halves(values * (2.0 * scale))
         x_ops[where, 0:width] = high
         x_ops[where, width : 2 * width] = low
         x_ops[where, 2 * width : 3 * width] = high
@@ -201,7 +198,7 @@
         values = y_all[here, :]
         norm = jnp.broadcast_to(jnp.sum(values * values, axis=1, keepdims=True), (count, LANES))
         y_norm[here, :] = norm
-        bias = across(a_col[here, :] - norm * (scale * LOG2E), wide_rows)
+        bias = across(a_col[here, :] - norm * (scale), wide_rows)
         high, low = halves(values)
         left = jnp.concatenate([high, high, low], axis=1)
         for begin in range(0, rows, wide_rows):
@@ -211,8 +208,8 @@
             scores = product + bias
             old = row_top[:, span]
             top = jnp.maximum(old, jnp.max(scores, axis=0, keepdims=True))
-            total = jnp.sum(jnp.exp2(scores - top), axis=0, keepdims=True)
-            row_sum[:, span] = row_sum[:, span] * jnp.exp2(old - top) + total
+            total = jnp.sum(jnp.exp(scores - top), axis=0, keepdims=True)
+            row_sum[:, span] = row_sum[:, span] * jnp.exp(old - top) + total
             row_top[:, span] = top
 
     def half_sweep(unit, carry):
@@ -250,15 +247,15 @@
             device_id_type=pl.DeviceIdType.MESH,
         )
 
-    row_parts[t] = row_top[...] + jnp.log2(row_sum[...])
+    row_parts[t] = row_top[...] + jnp.log(row_sum[...])
     for d in range(1, n_tgt):
         row_copy(d, t).start()
     norms = flat(x_norm[...])
     for d in range(1, n_tgt):
         row_copy(d, (t + n_tgt - d) % n_tgt).wait_recv()
     lse = combine(row_parts, n_tgt)
-    b_rows[...] = jnp.broadcast_to(log_src[...] * LOG2E - lse, b_rows.shape)
-    src_out[...] = norms / width - (EPSILON * LN2) * lse
+    b_rows[...] = jnp.broadcast_to(log_src[...] - lse, b_rows.shape)
+    src_out[...] = norms / width - EPSILON * lse
 
     group = min(256, cols // PARTS)
 
@@ -273,12 +270,12 @@
             ]
             top = functools.reduce(jnp.maximum, scores)
             tops.append(top)
-            totals.append(sum(jnp.exp2(score - top) for score in scores))
+            totals.append(sum(jnp.exp(score - top) for score in scores))
         lane_top = jnp.transpose(jnp.concatenate(tops, axis=0))
         lane_total = jnp.transpose(jnp.concatenate(totals, axis=0))
         top = jnp.max(lane_top, axis=0, keepdims=True)
-        total = jnp.sum(lane_total * jnp.exp2(lane_top - top), axis=0, keepdims=True)
-        col_parts[s, :, pl.ds(begin, group)] = top + jnp.log2(total)
+        total = jnp.sum(lane_total * jnp.exp(lane_top - top), axis=0, keepdims=True)
+        col_parts[s, :, pl.ds(begin, group)] = top + jnp.log(total)
         return carry
 
     share = cols // PARTS
@@ -310,7 +307,7 @@
 
     norms = flat(y_norm[...])
     lax.fori_loop(1, n_src, take_columns, 0)
-    tgt_out[...] = norms / width - (EPSILON * LN2) * combine(col_parts, n_src)
+    tgt_out[...] = norms / width - EPSILON * combine(col_parts, n_src)
 
     def settle_ring(k, carry):
         for way, c in order:

time: 70 us -> 70.2 us (level)
  no operation moved by 1% of the time
where the time goes in v5:
time: 70.2 us; the launch traced here: 70 us
  Pallas kernels  67.5 us (96%)
  local copies, waits for them, and re-layouts  1.91 us (3%)
    pallas_call x1, Pallas kernels, shards(): pl.pallas_call(functools.partial(kernel, n_src, n_tgt, wide, deep), out_s...  67.5 us
    unnamed x4, local copies, waits for them, and re-layouts  1.91 us

profile of v5, /device:TPU:0, one launch (start us, length us, event | category | flops | bytes accessed | tf_op | source)
XLA Modules:
  0.0 70.0 jit_solution(11119283167880617576)
XLA Ops:
  0.6 67.5 %shard_map.68 = (f32[1,2048]{1,0:T(1,128)}, f32[1,4096]{1,0:T(1,128)}) custom-call(f32[512,256]{1,0:T(8,128)} %x_own.1, f32[512,256]{1,0:T(8,128)} %y_own.1, f32[1,2048]{1,0:T(1,128)} %bitcast.9, f32[1,4096]{1,0:T(1,128)} %bitcast.7, f32[1,4096]{1,0:T(1,128)} %bitcast.8), custom_call_target="tpu_custom_call" | custom-call | flops 12884901888 | bytes 6291456 | tf_op jit(solution)/shard_map/pallas_call | solution.py:341
  68.1 0.0 copy-start
  68.1 1.3 %copy.9 = f32[2048]{0:T(1024)} copy(f32[2048]{0:T(1024)} %bitcast.6) | data formatting | bytes 16384
  69.4 0.0 copy-done
  69.4 0.6 copy.10
Async XLA Ops:
  68.1 1.3 %copy-start = (f32[1,4096]{1,0:T(1,128)S(1)}, f32[1,4096]{1,0:T(1,128)}, u32[]{:S(2)}) copy-start(f32[1,4096]{1,0:T(1,128)} %get-tuple-element.5) | copy-start | bytes 49156
